TPU v7x, 32 devices: a whole 2x2x4 slice. The times are simulated.
32 devices in a mesh: seq: 8 (over z, core), section: 4 (over y, x).
Axes of the slice: x: 2, y: 2, z: 4, core: 2. Of those that a mesh axis runs over, the one named last changes fastest.
Arguments:
- query: bfloat16 [4, 3072, 3072], P('section', 'seq'), may hold values from -24 to 24, as said below
- key: bfloat16 [4, 3072, 3072], P('section', 'seq'), may hold values from -24 to 24
- value: bfloat16 [4, 3072, 3072], P('section', 'seq'), may hold values from -6 to 6
- cotangent: bfloat16 [4, 3072, 3072], P('section', 'seq'), may hold values from -96 to 96
- adjacency: int32 [24, 9], P('seq'), may hold values from 0 to 1, as said below
Outputs:
- gradients: bfloat16 [4, 3072, 3, 3072], P('section', 'seq')
Inputs may be any that keep to these rules, and one draw needn't show every extreme that they name: query and key are drawn together. `adjacency`: the tile relation is symmetric: query tile a attends key tile b exactly when query tile b attends key tile a; every tile attends itself.
All inputs are finite; a program needn't handle non-finite values.
Results may differ from a plain program's by a relative error of at most 0.009.
Values may be sent and summed in bfloat16 or wider, within the bound.
No kernel may reach another device: no remote copies, remote signals or barrier semaphores. Data moves between devices by JAX's collectives and lax.ppermute only.
A program may use at most 128 MiB of HBM per device.

v0:
```python
import math

import jax
import jax.numpy as jnp
from jax import lax
from jax.sharding import PartitionSpec as P

HD = 128


def from_behind(block, axis, distance):
    devices = range(lax.axis_size(axis))
    route = [((i - distance) % len(devices), i) for i in devices]
    return lax.ppermute(block, axis, route)


def expand_mask(blocks, tile):
    count_rows, count_cols = blocks.shape
    wide = jnp.broadcast_to(blocks[:, None, :, None] > 0, (count_rows, tile, count_cols, tile))
    return wide.reshape(count_rows * tile, count_cols * tile)


def split_heads(matrix, start, group, head_dim):
    piece = lax.dynamic_slice_in_dim(matrix, start, group * head_dim, 1)
    return piece.reshape(matrix.shape[0], group, head_dim)


def masked_scores(queries, keys, mask, scale):
    scores = jnp.einsum("rgc,kgc->grk", queries, keys, preferred_element_type=jnp.float32) * scale
    return jnp.where(mask[None], scores, -jnp.inf)


def value_terms(prob, values, grads_out):
    prob_half = prob.astype(jnp.bfloat16)
    output = jnp.einsum("grk,kgc->rgc", prob_half, values, preferred_element_type=jnp.float32)
    delta = jnp.einsum("rgc,rgc->gr", grads_out.astype(jnp.float32), output)
    return (prob_half, delta)


def score_grads(prob, delta, values, grads_out):
    dprob = jnp.einsum("rgc,kgc->grk", grads_out, values, preferred_element_type=jnp.float32)
    return (prob * (dprob - delta[:, :, None])).astype(jnp.bfloat16)


def put_columns(target, piece, start):
    flat = piece.astype(jnp.bfloat16).reshape(piece.shape[0], piece.shape[1] * piece.shape[2])
    return lax.dynamic_update_slice_in_dim(target, flat, start, 1)


def per_device(query, key, value, cotangent, adjacency):
    queries = query[0]
    keys = key[0]
    values = value[0]
    grads_out = cotangent[0]
    rows, width = queries.shape
    head_dim = HD
    heads = width // head_dim
    group = math.gcd(heads, 4)
    group_width = group * head_dim
    groups = heads // group
    tiles_dev = adjacency.shape[0]
    tile = rows // tiles_dev
    scale = head_dim ** (-0.5)
    own_mask = expand_mask(adjacency, tile)
    blank = jnp.zeros((rows, width), jnp.bfloat16)
    keys_below, values_below = from_behind((keys, values), "seq", 1)
    keys_above, values_above = from_behind((keys, values), "seq", -1)
    window_keys = jnp.concatenate([keys_below, keys, keys_above], 0)
    window_values = jnp.concatenate([values_below, values, values_above], 0)
    blank_window = jnp.zeros((3 * rows, width), jnp.bfloat16)

    def full_step(index, carry):
        grad_query, part_key, part_value = carry
        start = index * group_width
        q_group = split_heads(queries, start, group, head_dim)
        o_group = split_heads(grads_out, start, group, head_dim)
        k_group = split_heads(window_keys, start, group, head_dim)
        v_group = split_heads(window_values, start, group, head_dim)
        scores = masked_scores(q_group, k_group, own_mask, scale)
        top = jnp.max(scores, axis=2)
        weight = jnp.exp(scores - top[:, :, None])
        prob = weight / jnp.sum(weight, axis=2)[:, :, None]
        prob_half, delta = value_terms(prob, v_group, o_group)
        dscore = score_grads(prob, delta, v_group, o_group)
        dquery = (
            jnp.einsum("grk,kgc->rgc", dscore, k_group, preferred_element_type=jnp.float32) * scale
        )
        dkey = (
            jnp.einsum("grk,rgc->kgc", dscore, q_group, preferred_element_type=jnp.float32) * scale
        )
        dvalue = jnp.einsum("grk,rgc->kgc", prob_half, o_group, preferred_element_type=jnp.float32)
        return (
            put_columns(grad_query, dquery, start),
            put_columns(part_key, dkey, start),
            put_columns(part_value, dvalue, start),
        )

    grad_query, part_key, part_value = lax.fori_loop(
        0, groups, full_step, (blank, blank_window, blank_window)
    )
    back_key, back_value = from_behind((part_key[:rows], part_value[:rows]), "seq", -1)
    ahead_key, ahead_value = from_behind((part_key[2 * rows :], part_value[2 * rows :]), "seq", 1)
    grad_key = (
        part_key[rows : 2 * rows].astype(jnp.float32)
        + back_key.astype(jnp.float32)
        + ahead_key.astype(jnp.float32)
    ).astype(jnp.bfloat16)
    grad_value = (
        part_value[rows : 2 * rows].astype(jnp.float32)
        + back_value.astype(jnp.float32)
        + ahead_value.astype(jnp.float32)
    ).astype(jnp.bfloat16)
    packed = jnp.stack([grad_query, grad_key, grad_value], axis=1)[None]
    return from_behind(packed, "section", -1)


def solution(mesh):
    in_specs = (
        P("section", "seq", None),
        P("section", "seq", None),
        P("section", "seq", None),
        P("section", "seq", None),
        P("seq", None),
    )
    out_specs = P("section", "seq", None, None)
    return jax.shard_map(
        per_device, mesh=mesh, in_specs=in_specs, out_specs=out_specs, check_vma=False
    )
```

profile of v0, /device:TPU:31, one launch (start us, length us, event | category | flops | bytes accessed | tf_op | source)
XLA Modules:
  0.0 572.0 jit_solution(15710247607399299506)
XLA Ops:
  0.0 4.3 copy.24
  4.9 2.9 collective-permute-start.2
  7.8 3.0 copy.21
  10.9 3.5 collective-permute-start
  14.5 4.3 copy.22
  18.8 4.3 copy.23
  23.1 36.9 %collective-permute-done.3 = bf16[384,3072]{0,1:T(8,128)(2,1)} collective-permute-done((bf16[384,3072]{0,1:T(8,128)(2,1)}, bf16[384,3072]{0,1:T(8,128)(2,1)}, u32[]{:S(2)}, u32[]{:S(2)}) %collective-permute-start.3) | collective-permute-done | bytes 2359328 | tf_op jit(solution)/shard_map/ppermute | solution.py:14
  60.0 6.3 %pad_maximum_fusion.1 = bf16[1152,3072]{0,1:T(8,128)(2,1)} fusion(bf16[384,3072]{0,1:T(8,128)(2,1)} %collective-permute-done.3, bf16[384,3072]{0,1:T(8,128)(2,1)} %bitcast.5, bf16[384,3072]{0,1:T(8,128)(2,1)} %collective-permute-done.2), kind=kLoop, calls=%fused_computation.31 | loop fusion | flops 21233664 | bytes 14155776 | tf_op jit(solution)/shard_map/concatenate | solution.py:69
  66.3 42.3 %collective-permute-done.1 = bf16[384,3072]{0,1:T(8,128)(2,1)} collective-permute-done((bf16[384,3072]{0,1:T(8,128)(2,1)S(1)}, bf16[384,3072]{0,1:T(8,128)(2,1)}, u32[]{:S(2)}, u32[]{:S(2)}) %collective-permute-start.1) | collective-permute-done | bytes 2359328 | tf_op jit(solution)/shard_map/ppermute | solution.py:14
  108.6 5.8 %pad_maximum_fusion = bf16[1152,3072]{0,1:T(8,128)(2,1)} fusion(bf16[384,3072]{0,1:T(8,128)(2,1)} %collective-permute-done.1, bf16[384,3072]{0,1:T(8,128)(2,1)S(1)} %bitcast.115, bf16[384,3072]{0,1:T(8,128)(2,1)} %collective-permute-done), kind=kLoop, calls=%fused_computation.30 | loop fusion | flops 21233664 | bytes 14155776 | tf_op jit(solution)/shard_map/concatenate | solution.py:68
  116.0 3.7 broadcast_in_dim.53.clone2
  119.7 3.8 broadcast_in_dim.53.clone
  123.6 181.3 %while.18 = (s32[]{:T(128)}, bf16[384,3072]{1,0:T(8,128)(2,1)}, bf16[1152,3072]{1,0:T(8,128)(2,1)}, bf16[1152,3072]{1,0:T(8,128)(2,1)}, bf16[1152,3072]{0,1:T(8,...) while((s32[]{:T(128)}, bf16[384,3072]{1,0:T(8,128)(2,1)}, ...), condition=%wide.region_3.4_spmd.clone, body=%wide.region_0.3_spmd.clone.sunk | while | flops 2738355712 | bytes 100202736 | solution.py:98
  130.6 6.5 %fusion.62 = (f32[4,384]{1,0:T(4,128)S(1)}, f32[4,384,1152]{2,1,0:T(8,128)}) fusion(pred[384,1152]{1,0:T(8,128)(4,1)} %copy.59, bf16[384,4,128]{0,2,1:T(8,128)(2,1)S(1)} %bitcast.108, bf16[1152,4,128]{0,2,1:T(8,128)(2,1)S(1)} %bitcast.104), kind=kOutput, calls=%fused_computation.38.clone.1 | convolution fusion | flops 460063872 | bytes 9099264 | tf_op jit(solution)/shard_map/while/body/eval_jaxpr/sub | solution.py:81
  137.1 3.9 fusion.63
  160.8 6.5 %fusion.62 = (f32[4,384]{1,0:T(4,128)S(1)}, f32[4,384,1152]{2,1,0:T(8,128)}) fusion(pred[384,1152]{1,0:T(8,128)(4,1)} %copy.59, bf16[384,4,128]{0,2,1:T(8,128)(2,1)S(1)} %bitcast.108, bf16[1152,4,128]{0,2,1:T(8,128)(2,1)S(1)} %bitcast.104), kind=kOutput, calls=%fused_computation.38.clone.1 | convolution fusion | flops 460063872 | bytes 9099264 | tf_op jit(solution)/shard_map/while/body/eval_jaxpr/sub | solution.py:81
  167.3 3.9 fusion.63
  191.0 6.5 %fusion.62 = (f32[4,384]{1,0:T(4,128)S(1)}, f32[4,384,1152]{2,1,0:T(8,128)}) fusion(pred[384,1152]{1,0:T(8,128)(4,1)} %copy.59, bf16[384,4,128]{0,2,1:T(8,128)(2,1)S(1)} %bitcast.108, bf16[1152,4,128]{0,2,1:T(8,128)(2,1)S(1)} %bitcast.104), kind=kOutput, calls=%fused_computation.38.clone.1 | convolution fusion | flops 460063872 | bytes 9099264 | tf_op jit(solution)/shard_map/while/body/eval_jaxpr/sub | solution.py:81
  197.5 3.9 fusion.63
  221.2 6.5 %fusion.62 = (f32[4,384]{1,0:T(4,128)S(1)}, f32[4,384,1152]{2,1,0:T(8,128)}) fusion(pred[384,1152]{1,0:T(8,128)(4,1)} %copy.59, bf16[384,4,128]{0,2,1:T(8,128)(2,1)S(1)} %bitcast.108, bf16[1152,4,128]{0,2,1:T(8,128)(2,1)S(1)} %bitcast.104), kind=kOutput, calls=%fused_computation.38.clone.1 | convolution fusion | flops 460063872 | bytes 9099264 | tf_op jit(solution)/shard_map/while/body/eval_jaxpr/sub | solution.py:81
  227.7 3.9 fusion.63
  251.4 6.5 %fusion.62 = (f32[4,384]{1,0:T(4,128)S(1)}, f32[4,384,1152]{2,1,0:T(8,128)}) fusion(pred[384,1152]{1,0:T(8,128)(4,1)} %copy.59, bf16[384,4,128]{0,2,1:T(8,128)(2,1)S(1)} %bitcast.108, bf16[1152,4,128]{0,2,1:T(8,128)(2,1)S(1)} %bitcast.104), kind=kOutput, calls=%fused_computation.38.clone.1 | convolution fusion | flops 460063872 | bytes 9099264 | tf_op jit(solution)/shard_map/while/body/eval_jaxpr/sub | solution.py:81
  257.9 3.9 fusion.63
  281.7 6.5 %fusion.62 = (f32[4,384]{1,0:T(4,128)S(1)}, f32[4,384,1152]{2,1,0:T(8,128)}) fusion(pred[384,1152]{1,0:T(8,128)(4,1)} %copy.59, bf16[384,4,128]{0,2,1:T(8,128)(2,1)S(1)} %bitcast.108, bf16[1152,4,128]{0,2,1:T(8,128)(2,1)S(1)} %bitcast.104), kind=kOutput, calls=%fused_computation.38.clone.1 | convolution fusion | flops 460063872 | bytes 9099264 | tf_op jit(solution)/shard_map/while/body/eval_jaxpr/sub | solution.py:81
  288.2 3.9 fusion.63
  304.8 2.9 fusion.20
  311.7 3.5 collective-permute-start.5
  315.2 47.9 %collective-permute-done.6 = bf16[384,3072]{1,0:T(8,128)(2,1)S(1)} collective-permute-done((bf16[384,3072]{1,0:T(8,128)(2,1)S(1)}, bf16[384,3072]{1,0:T(8,128)(2,1)S(1)}, u32[]{:S(2)}, u32[]{:S(2)}) %collective-permute-start.6) | collective-permute-done | bytes 2359328 | tf_op jit(solution)/shard_map/ppermute | solution.py:14
  363.1 2.9 fusion.17
  366.0 46.7 %collective-permute-done.4 = bf16[384,3072]{1,0:T(8,128)(2,1)S(1)} collective-permute-done((bf16[384,3072]{1,0:T(8,128)(2,1)S(1)}, bf16[384,3072]{1,0:T(8,128)(2,1)S(1)}, u32[]{:S(2)}, u32[]{:S(2)}) %collective-permute-start.4) | collective-permute-done | bytes 2359328 | tf_op jit(solution)/shard_map/ppermute | solution.py:14
  415.1 153.9 %collective-permute-done.8 = bf16[1,384,3,3072]{3,1,2,0:T(8,128)(2,1)S(1)} collective-permute-done((bf16[1,384,3,3072]{3,1,2,0:T(8,128)(2,1)S(1)}, bf16[1,384,3,3072]{3,1,2,0:T(8,128)(2,1)S(1)}, u32[]{:S(2)}, u32[]{:S(2)}) %collective-permute-start.8) | collective-permute-done | bytes 7077920 | tf_op jit(solution)/shard_map/ppermute | solution.py:14
  569.0 3.0 copy.79
  (136 shorter events, 127.5 us)
Async XLA Ops:
  4.3 10.1 %copy-start.3 = (s32[3,9]{1,0:T(4,128)S(1)}, s32[3,9]{1,0:T(4,128)}, u32[]{:S(2)}) copy-start(s32[3,9]{1,0:T(4,128)} %param.11) | copy-start | bytes 328
  4.3 55.7 %collective-permute-start.3 = (bf16[384,3072]{0,1:T(8,128)(2,1)}, bf16[384,3072]{0,1:T(8,128)(2,1)}, u32[]{:S(2)}, u32[]{:S(2)}) collective-permute-start(bf16[384,3072]{0,1:T(8,128)(2,1)} %bitcast.5), channel_id=1, source_target_pairs={{4,0},{8,4},{12,8},{16,12},{20,16},{24,20},{28,24},{0,28},{5,1},{9... | collective-permute-start | bytes 7077896 | tf_op jit(solution)/shard_map/ppermute | solution.py:14
  4.9 55.1 %collective-permute-start.2 = (bf16[384,3072]{0,1:T(8,128)(2,1)}, bf16[384,3072]{0,1:T(8,128)(2,1)}, u32[]{:S(2)}, u32[]{:S(2)}) collective-permute-start(bf16[384,3072]{0,1:T(8,128)(2,1)} %bitcast.5), channel_id=1, source_target_pairs={{28,0},{0,4},{4,8},{8,12},{12,16},{16,20},{20,24},{24,28},{29,1},{... | collective-permute-start | bytes 7077896 | tf_op jit(solution)/shard_map/ppermute | solution.py:14
  10.8 97.8 %collective-permute-start.1 = (bf16[384,3072]{0,1:T(8,128)(2,1)S(1)}, bf16[384,3072]{0,1:T(8,128)(2,1)}, u32[]{:S(2)}, u32[]{:S(2)}) collective-permute-start(bf16[384,3072]{0,1:T(8,128)(2,1)S(1)} %bitcast.113), channel_id=1, source_target_pairs={{4,0},{8,4},{12,8},{16,12},{20,16},{24,20},{28,24},{0,28},{5,1},{9... | collective-permute-start | bytes 7077896 | tf_op jit(solution)/shard_map/ppermute | solution.py:14
  10.9 97.7 %collective-permute-start = (bf16[384,3072]{0,1:T(8,128)(2,1)S(1)}, bf16[384,3072]{0,1:T(8,128)(2,1)}, u32[]{:S(2)}, u32[]{:S(2)}) collective-permute-start(bf16[384,3072]{0,1:T(8,128)(2,1)S(1)} %bitcast.114), channel_id=1, source_target_pairs={{28,0},{0,4},{4,8},{8,12},{12,16},{16,20},{20,24},{24,28},{29,1},{... | collective-permute-start | bytes 7077896 | tf_op jit(solution)/shard_map/ppermute | solution.py:14
  137.1 5.0 copy-start
  167.3 5.0 copy-start
  197.5 5.0 copy-start
  227.7 5.0 copy-start
  257.9 5.0 copy-start
  288.2 5.0 copy-start
  304.8 6.5 %copy-start.1 = (bf16[1152,3072]{1,0:T(8,128)(2,1)S(1)}, bf16[1152,3072]{1,0:T(8,128)(2,1)}, u32[]{:S(2)}) copy-start(bf16[1152,3072]{1,0:T(8,128)(2,1)} %get-tuple-element.162) | copy-start | bytes 21233668
  307.7 55.4 %collective-permute-start.6 = (bf16[384,3072]{1,0:T(8,128)(2,1)S(1)}, bf16[384,3072]{1,0:T(8,128)(2,1)S(1)}, u32[]{:S(2)}, u32[]{:S(2)}) collective-permute-start(bf16[384,3072]{1,0:T(8,128)(2,1)S(1)} %get-tuple-element.209), channel_id=1, source_target_pairs={{4,0},{8,4},{12,8},{16,12},{20,16},{24,20},{28,24},{0,28},{5,1},{9... | collective-permute-start | bytes 7077896 | tf_op jit(solution)/shard_map/ppermute | solution.py:14
  308.5 54.6 %collective-permute-start.7 = (bf16[384,3072]{1,0:T(8,128)(2,1)S(1)}, bf16[384,3072]{1,0:T(8,128)(2,1)S(1)}, u32[]{:S(2)}, u32[]{:S(2)}) collective-permute-start(bf16[384,3072]{1,0:T(8,128)(2,1)S(1)} %get-tuple-element.210), channel_id=1, source_target_pairs={{28,0},{0,4},{4,8},{8,12},{12,16},{16,20},{20,24},{24,28},{29,1},{... | collective-permute-start | bytes 7077896 | tf_op jit(solution)/shard_map/ppermute | solution.py:14
  311.6 101.0 %collective-permute-start.4 = (bf16[384,3072]{1,0:T(8,128)(2,1)S(1)}, bf16[384,3072]{1,0:T(8,128)(2,1)S(1)}, u32[]{:S(2)}, u32[]{:S(2)}) collective-permute-start(bf16[384,3072]{1,0:T(8,128)(2,1)S(1)} %get-tuple-element.207), channel_id=1, source_target_pairs={{4,0},{8,4},{12,8},{16,12},{20,16},{24,20},{28,24},{0,28},{5,1},{9... | collective-permute-start | bytes 7077896 | tf_op jit(solution)/shard_map/ppermute | solution.py:14
  311.7 101.0 %collective-permute-start.5 = (bf16[384,3072]{1,0:T(8,128)(2,1)S(1)}, bf16[384,3072]{1,0:T(8,128)(2,1)S(1)}, u32[]{:S(2)}, u32[]{:S(2)}) collective-permute-start(bf16[384,3072]{1,0:T(8,128)(2,1)S(1)} %get-tuple-element.208), channel_id=1, source_target_pairs={{28,0},{0,4},{4,8},{8,12},{12,16},{16,20},{20,24},{24,28},{29,1},{... | collective-permute-start | bytes 7077896 | tf_op jit(solution)/shard_map/ppermute | solution.py:14
  366.0 47.9 %copy-start.2 = (bf16[384,3072]{1,0:T(8,128)(2,1)S(1)}, bf16[384,3072]{1,0:T(8,128)(2,1)}, u32[]{:S(2)}) copy-start(bf16[384,3072]{1,0:T(8,128)(2,1)} %get-tuple-element.161) | copy-start | bytes 7077892
  414.8 154.2 %collective-permute-start.8 = (bf16[1,384,3,3072]{3,1,2,0:T(8,128)(2,1)S(1)}, bf16[1,384,3,3072]{3,1,2,0:T(8,128)(2,1)S(1)}, u32[]{:S(2)}, u32[]{:S(2)}) collective-permute-start(bf16[1,384,3,3072]{3,1,2,0:T(8,128)(2,1)S(1)} %maximum_bitcast_fusion), channel_id=1, source_target_pairs={{1,0},{2,1},{3,2},{0,3},{5,4},{6,5},{7,6},{4,7},{9,8},{10,9},{11,1... | collective-permute-start | bytes 21233672 | tf_op jit(solution)/shard_map/ppermute | solution.py:14
where the time goes:
time: 574 us; the launch traced here: 572 us
  waiting for transfers between devices  328 us (57%)
  local copies, waits for them, and re-layouts  112 us (20%)
  matrix products  76.8 us (13%)
  other arithmetic  40.2 us (7%)
  starting transfers between devices  14.6 us (3%)
    ppermute x9, waiting for transfers between devices, from_behind(): return lax.ppermute(block, axis, route)  328 us
    sub x6, matrix products, full_step(): weight = jnp.exp(scores - top[:, :, None])  39 us
    dynamic_update_slice x30, local copies, waits for them, and re-layouts, put_columns(): return lax.dynamic_update_slice_in_dim(target, flat, start, 1)  39 us
    dynamic_slice x24, local copies, waits for them, and re-layouts, split_heads(): piece = lax.dynamic_slice_in_dim(matrix, start, group * head_dim, 1)  28.8 us
    convert_element_type x6, other arithmetic, value_terms(): prob_half = prob.astype(jnp.bfloat16)  23.1 us
    unnamed x12, local copies, waits for them, and re-layouts  18.9 us
    ppermute x9, starting transfers between devices, from_behind(): return lax.ppermute(block, axis, route)  14.6 us
  transfers between devices with their start and end apart: 9, of which 5 were waited for; matrix products, arithmetic and copies ran while one was open for 4% of the time, Pallas kernels for 0%

commit v1 on v0

v1 whole, which is shorter than its diff:
```python
import functools
import math

import jax
import jax.numpy as jnp
from jax import lax
from jax.experimental import pallas as pl
from jax.experimental.pallas import tpu as pltpu
from jax.sharding import PartitionSpec as P

HD = 128
MASKED = 1e30
LOG2E = math.log2(math.e)
VMEM = 24 * 1024 * 1024


def nt(left, right):
    return lax.dot_general(left, right, (((1,), (1,)), ((), ())), preferred_element_type=jnp.float32)


def nn(left, right):
    return lax.dot_general(left, right, (((1,), (0,)), ((), ())), preferred_element_type=jnp.float32)


def stats_kernel(group, tiles, scale, bias, q_own, o_own, near, far, key, value, st_near, st_own, st_far):
    head = pl.program_id(0)
    keys = key[0]
    values = value[0]
    tile = keys.shape[0] // tiles
    windows = ((near[0], near[1], st_near), (q_own[0], o_own[0], st_own), (far[0], far[1], st_far))
    for w, (queries, grads, out) in enumerate(windows):
        scores = nt(keys, queries)
        dprob = nt(values, grads)
        shut = [bias[w * tiles + j : w * tiles + j + 1, :] for j in range(tiles)]
        parts = [scores[j * tile : (j + 1) * tile] for j in range(tiles)]
        top = None
        for j in range(tiles):
            best = jnp.max(parts[j], axis=0, keepdims=True) * scale - shut[j]
            top = best if top is None else jnp.maximum(top, best)
        total = jnp.zeros_like(top)
        moment = jnp.zeros_like(top)
        for j in range(tiles):
            row = jnp.where(shut[j] > 0.0, MASKED, top)
            weight = jnp.exp2(parts[j] * scale - row)
            total = total + jnp.sum(weight, axis=0, keepdims=True)
            moment = moment + jnp.sum(weight * dprob[j * tile : (j + 1) * tile], axis=0, keepdims=True)
        some = total > 0.0
        safe = jnp.where(some, total, 1.0)
        out[pl.ds(head, 1), :] = jnp.where(some, top + jnp.log2(safe), -MASKED)
        out[pl.ds(group + head, 1), :] = jnp.where(some, moment / safe, 0.0)


def grads_kernel(
    group, tiles, scale, out_scale, bias, q_own, o_own, near, far, key, value, st_near, st_own, st_far,
    dq_near, dq_own, dq_far, dkv, prob_all, dscore_all
):
    head = pl.program_id(0)
    keys = key[0]
    values = value[0]
    rows = keys.shape[0]
    tile = rows // tiles
    windows = ((near[0], near[1], st_near, dq_near), (q_own[0], o_own[0], st_own, dq_own), (far[0], far[1], st_far, dq_far))
    for w, (queries, grads, stat, dq) in enumerate(windows):
        scores = nt(keys, queries)
        dprob = nt(values, grads)
        lse = stat[pl.ds(head, 1), :]
        delta = stat[pl.ds(group + head, 1), :]
        for j in range(tiles):
            span = slice(j * tile, (j + 1) * tile)
            row = lse + bias[w * tiles + j : w * tiles + j + 1, :]
            prob = jnp.exp2(scores[span] * scale - row)
            prob_all[span, w * rows : (w + 1) * rows] = prob.astype(jnp.bfloat16)
            dscore_all[span, w * rows : (w + 1) * rows] = (prob * (dprob[span] - delta)).astype(jnp.bfloat16)
        back = lax.dot_general(
            dscore_all[:, w * rows : (w + 1) * rows], keys, (((0,), (0,)), ((), ())),
            preferred_element_type=jnp.float32,
        )
        dq[...] = (back * out_scale).astype(dq.dtype)
    dkey = None
    dvalue = None
    for w, (queries, grads, stat, dq) in enumerate(windows):
        part = nn(dscore_all[:, w * rows : (w + 1) * rows], queries)
        dkey = part if dkey is None else dkey + part
        part = nn(prob_all[:, w * rows : (w + 1) * rows], grads)
        dvalue = part if dvalue is None else dvalue + part
    dkv[0] = (dkey * out_scale).astype(jnp.bfloat16)
    dkv[1] = dvalue.astype(jnp.bfloat16)


def head_spec(rows, lead, first):
    return pl.BlockSpec((1, rows, HD), lambda h: (lead, 0, first + h))


def whole_spec(shape):
    return pl.BlockSpec(shape, lambda h: (0,) * len(shape))


def input_specs(bias, near, places, group):
    rows = near.shape[1]
    pair = pl.BlockSpec((2, rows, HD), lambda h: (0, 0, h))
    own = [head_spec(rows, lead, first) for lead, first in places]
    return [whole_spec(bias.shape), own[0], own[1], pair, pair, own[2], own[3]]


def window_stats(bias, arrays, places, near, far, group):
    rows = near.shape[1]
    tiles = bias.shape[0] // 3
    scale = HD ** (-0.5) * LOG2E
    stat = jax.ShapeDtypeStruct((2 * group, rows), jnp.float32)
    return pl.pallas_call(
        functools.partial(stats_kernel, group, tiles, scale),
        grid=(group,),
        in_specs=input_specs(bias, near, places, group),
        out_specs=[whole_spec(stat.shape)] * 3,
        out_shape=[stat] * 3,
        compiler_params=pltpu.CompilerParams(vmem_limit_bytes=VMEM),
        cost_estimate=pl.CostEstimate(
            flops=group * 2 * 2 * 3 * rows * rows * HD,
            bytes_accessed=group * 8 * rows * HD * 2,
            transcendentals=group * 3 * rows * rows,
        ),
        name="window_stats",
    )(bias, arrays[0], arrays[1], near, far, arrays[2], arrays[3])


def window_grads(bias, arrays, places, near, far, stats, group):
    rows = near.shape[1]
    tiles = bias.shape[0] // 3
    scale = HD ** (-0.5) * LOG2E
    width = group * HD
    flat = pl.BlockSpec((rows, HD), lambda h: (0, h))
    return pl.pallas_call(
        functools.partial(grads_kernel, group, tiles, scale, HD ** (-0.5)),
        grid=(group,),
        in_specs=input_specs(bias, near, places, group) + [whole_spec(stats[0].shape)] * 3,
        out_specs=[flat, flat, flat, pl.BlockSpec((2, rows, HD), lambda h: (0, 0, h))],
        out_shape=[
            jax.ShapeDtypeStruct((rows, width), jnp.bfloat16),
            jax.ShapeDtypeStruct((rows, width), jnp.float32),
            jax.ShapeDtypeStruct((rows, width), jnp.bfloat16),
            jax.ShapeDtypeStruct((2, rows, width), jnp.bfloat16),
        ],
        scratch_shapes=[pltpu.VMEM((rows, 3 * rows), jnp.bfloat16)] * 2,
        compiler_params=pltpu.CompilerParams(vmem_limit_bytes=VMEM),
        cost_estimate=pl.CostEstimate(
            flops=group * 5 * 2 * 3 * rows * rows * HD,
            bytes_accessed=group * 14 * rows * HD * 2,
            transcendentals=group * 3 * rows * rows,
        ),
        name="window_grads",
    )(bias, arrays[0], arrays[1], near, far, arrays[2], arrays[3], *stats)


def swap_near(block):
    size = lax.axis_size("seq")
    return lax.ppermute(block, "seq", [(i, i ^ 1) for i in range(size)])


def swap_far(block):
    size = lax.axis_size("seq")
    return lax.ppermute(block, "seq", [(i, (i + 1 if i % 2 else i - 1) % size) for i in range(size)])


def to_previous(block):
    size = lax.axis_size("section")
    return lax.ppermute(block, "section", [((i + 1) % size, i) for i in range(size)])


def merge(own, near, far, group):
    lse = [part[:group] for part in (own, near, far)]
    mean = [part[group:] for part in (own, near, far)]
    top = jnp.maximum(lse[0], jnp.maximum(lse[1], lse[2]))
    weight = [jnp.exp2(part - top) for part in lse]
    total = weight[0] + weight[1] + weight[2]
    delta = (weight[0] * mean[0] + weight[1] * mean[1] + weight[2] * mean[2]) / total
    return jnp.concatenate([top + jnp.log2(total), delta], 0)


def tile_bias(adjacency, tile):
    tiles = adjacency.shape[0]
    blocks = adjacency.reshape(tiles, 3, tiles)
    odd = lax.axis_index("seq") % 2 == 1
    near = jnp.where(odd, blocks[:, 0], blocks[:, 2])
    far = jnp.where(odd, blocks[:, 2], blocks[:, 0])
    flags = jnp.concatenate([near, blocks[:, 1], far], 0)
    bias = jnp.where(flags > 0, 0.0, MASKED).astype(jnp.float32)
    return jnp.repeat(bias, tile, axis=1)


def per_device(query, key, value, cotangent, adjacency):
    rows, width = query.shape[1:]
    heads = width // HD
    moved = heads // 6
    size = heads // 6
    first_moved = heads - moved
    local = [(s, min(size, first_moved - s)) for s in range(0, first_moved, size)]
    bias = tile_bias(adjacency, rows // adjacency.shape[0])

    def columns(array, first, count):
        return array[:, :, first * HD : (first + count) * HD]

    pairs = [jnp.concatenate([columns(query, s, n), columns(cotangent, s, n)], 0) for s, n in local]
    groups = [((query, cotangent, key, value), ((0, s),) * 4, n) for s, n in local]
    qd_moved = to_previous(jnp.concatenate([columns(query, first_moved, moved), columns(cotangent, first_moved, moved)], 0))
    kv_moved = to_previous(jnp.concatenate([columns(key, first_moved, moved), columns(value, first_moved, moved)], 0))
    pairs.append(qd_moved)
    groups.append(((qd_moved, qd_moved, kv_moved, kv_moved), ((0, 0), (1, 0), (0, 0), (1, 0)), moved))

    count = len(groups)
    near = [swap_near(pair) for pair in pairs]
    far = [swap_far(pair) for pair in pairs]
    out = jnp.zeros((3, rows, width), jnp.bfloat16)
    pieces = []
    for g in range(count):
        arrays, places, n = groups[g]
        st_near, st_own, st_far = window_stats(bias, arrays, places, near[g], far[g], n)
        own = merge(st_own, swap_near(st_near), swap_far(st_far), n)
        stats = (swap_near(own), own, swap_far(own))
        dq_near, dq_own, dq_far, dkv = window_grads(bias, arrays, places, near[g], far[g], stats, n)
        dq = dq_own + swap_near(dq_near).astype(jnp.float32) + swap_far(dq_far).astype(jnp.float32)
        dq = dq.astype(jnp.bfloat16)[None]
        if g < count - 1:
            dkv = to_previous(dkv)
            dq = to_previous(dq)
        pieces.append(jnp.concatenate([dq, dkv], 0))
    out = jnp.concatenate(pieces, 2)
    return jnp.transpose(out, (1, 0, 2))[None]


def solution(mesh):
    in_specs = (
        P("section", "seq", None),
        P("section", "seq", None),
        P("section", "seq", None),
        P("section", "seq", None),
        P("seq", None),
    )
    out_specs = P("section", "seq", None, None)
    return jax.shard_map(
        per_device, mesh=mesh, in_specs=in_specs, out_specs=out_specs, check_vma=False
    )
```

time: 574 us -> 339 us (0.59)
  waiting for transfers between devices: 328 us -> 180 us
  local copies, waits for them, and re-layouts: 112 us -> 12.4 us
  Pallas kernels: 0 us -> 81.5 us
  matrix products: 76.8 us -> 0 us
  starting transfers between devices: 14.6 us -> 51 us
  other arithmetic: 40.2 us -> 9.03 us
    ppermute x9 -> x60, waiting for transfers between devices: 328 us -> 180 us  [the longest x12 93.1 us: to_previous(): lax.ppermute(block, 'section', [((i + 1) % size, i) for i in range(size)])]
    pallas_call x0 -> x12, Pallas kernels: none -> 81.5 us  [the longest x6 53.1 us: window_grads(): pl.pallas_call(functools.partial(grads_kernel, group, tiles, scale, HD **...]
    sub x6 -> x0, matrix products: 39 us -> none  [full_step(): weight = jnp.exp(scores - top[:, :, None])]
    dynamic_update_slice x30 -> x0, local copies, waits for them, and re-layouts: 39 us -> none  [put_columns(): return lax.dynamic_update_slice_in_dim(target, flat, start, 1)]
    dot_general x30 -> x0, matrix products: 37.7 us -> none  [the longest x6 11.3 us: full_step(): jnp.einsum('grk,kgc->rgc', dscore, k_group, preferred_element_type=jnp.fl...]
    ppermute x9 -> x60, starting transfers between devices: 14.6 us -> 51 us  [the longest x24 39 us: swap_far(): lax.ppermute(block, 'seq', [(i, (i + 1 if i % 2 else i - 1) % size) for i...]
    dynamic_slice x24 -> x0, local copies, waits for them, and re-layouts: 28.8 us -> none  [split_heads(): piece = lax.dynamic_slice_in_dim(matrix, start, group * head_dim, 1)]
    convert_element_type x6 -> x0, other arithmetic: 23.1 us -> none  [value_terms(): prob_half = prob.astype(jnp.bfloat16)]
  transfers between devices with their start and end apart: 9 -> 60, of which waited for: 5 -> 19; matrix products, arithmetic and copies ran while one was open for 4% -> 3% of each run, Pallas kernels for 0% -> 24%
where the time goes in v1:
time: 339 us; the launch traced here: 334 us
  waiting for transfers between devices  180 us (53%)
  Pallas kernels  81.5 us (24%)
  starting transfers between devices  51 us (15%)
  local copies, waits for them, and re-layouts  12.4 us (4%)
  other arithmetic  9.03 us (3%)
    ppermute x12, waiting for transfers between devices, to_previous(): lax.ppermute(block, 'section', [((i + 1) % size, i) for i in range(size)])  93.1 us
    ppermute x24, waiting for transfers between devices, swap_far(): lax.ppermute(block, 'seq', [(i, (i + 1 if i % 2 else i - 1) % size) for i...  85.9 us
    pallas_call x6, Pallas kernels, window_grads(): pl.pallas_call(functools.partial(grads_kernel, group, tiles, scale, HD **...  53.1 us
    ppermute x24, starting transfers between devices, swap_far(): lax.ppermute(block, 'seq', [(i, (i + 1 if i % 2 else i - 1) % size) for i...  39 us
    pallas_call x6, Pallas kernels, window_stats(): pl.pallas_call(functools.partial(stats_kernel, group, tiles, scale), grid...  28.4 us
    unnamed x18, local copies, waits for them, and re-layouts  7.81 us
    ppermute x12, starting transfers between devices, to_previous(): lax.ppermute(block, 'section', [((i + 1) % size, i) for i in range(size)])  7.04 us
  transfers between devices with their start and end apart: 60, of which 19 were waited for; matrix products, arithmetic and copies ran while one was open for 3% of the time, Pallas kernels for 24%

profile of v1, /device:TPU:31, one launch (start us, length us, event | category | flops | bytes accessed | tf_op | source)
XLA Modules:
  0.0 334.3 jit_solution(16976905476673715975)
XLA Ops:
  0.0 3.4 %fusion.25 = (bf16[1,384,512]{2,1,0:T(8,128)(2,1)S(1)}, bf16[1,384,512]{2,1,0:T(8,128)(2,1)S(1)}, bf16[1,384,512]{2,1,0:T(8,128)(2,1)S(1)}, bf16[1,384,512]{2,1,...) fusion(bf16[1,384,3072]{2,1,0:T(8,128)(2,1)} %q_own.19, ...), kind=kLoop, calls=%fused_computation.101 | loop fusion | bytes 9437184 | tf_op jit(solution)/shard_map/slice | solution.py:200
  6.5 3.0 collective-permute-start.11
  14.0 13.0 %collective-permute-done.1.far = bf16[2,384,512]{2,1,0:T(8,128)(2,1)} collective-permute-done((bf16[2,384,512]{2,1,0:T(8,128)(2,1)}, bf16[2,384,512]{2,1,0:T(8,128)(2,1)}, u32[]{:S(2)}, u32[]{:S(2)}) %collective-permute-start.1) | collective-permute-done | bytes 786464 | tf_op jit(solution)/shard_map/ppermute | solution.py:161
  27.1 16.8 %collective-permute-done.11.far = bf16[2,384,512]{2,1,0:T(8,128)(2,1)} collective-permute-done((bf16[2,384,512]{2,1,0:T(8,128)(2,1)}, bf16[2,384,512]{2,1,0:T(8,128)(2,1)}, u32[]{:S(2)}, u32[]{:S(2)}) %collective-permute-start.11) | collective-permute-done | bytes 786464 | tf_op jit(solution)/shard_map/ppermute | solution.py:161
  51.0 4.8 %window_stats.6 = (f32[8,384]{1,0:T(8,128)S(1)}, f32[8,384]{1,0:T(8,128)S(1)}, f32[8,384]{1,0:T(8,128)S(1)}) custom-call(f32[9,384]{1,0:T(8,128)S(1)} %bitcast.21, bf16[1,384,3072]{2,1,0:T(8,128)(2,1)S(1)} %copy-done, bf16[1,384,3072]{2,1,0:T(8,128)(2,1)S(1)} %copy-done.1, bf16[2,384,512]{2,1,0:T(8,128)(2,1)S(1)} %copy-done.5, ...), custom_call_target="tpu_custom_call" | custom-call | flops 905969664 | bytes 3145728 | tf_op jit(solution)/shard_map/window_stats/pallas_call | solution.py:110
  55.8 4.9 %window_stats.7 = (f32[8,384]{1,0:T(8,128)S(1)}, f32[8,384]{1,0:T(8,128)S(1)}, f32[8,384]{1,0:T(8,128)S(1)}) custom-call(f32[9,384]{1,0:T(8,128)S(1)} %bitcast.22, bf16[1,384,3072]{2,1,0:T(8,128)(2,1)S(1)} %copy-done, bf16[1,384,3072]{2,1,0:T(8,128)(2,1)S(1)} %copy-done.1, bf16[2,384,512]{2,1,0:T(8,128)(2,1)} %collective-permute-done.10.near, ...), custom_call_target="tpu_custom_call" | custom-call | flops 905969664 | bytes 3145728 | tf_op jit(solution)/shard_map/window_stats/pallas_call | solution.py:110
  61.0 4.9 %window_stats.8 = (f32[8,384]{1,0:T(8,128)S(1)}, f32[8,384]{1,0:T(8,128)S(1)}, f32[8,384]{1,0:T(8,128)S(1)}) custom-call(f32[9,384]{1,0:T(8,128)S(1)} %bitcast.23, bf16[1,384,3072]{2,1,0:T(8,128)(2,1)S(1)} %copy-done, bf16[1,384,3072]{2,1,0:T(8,128)(2,1)S(1)} %copy-done.1, bf16[2,384,512]{2,1,0:T(8,128)(2,1)} %collective-permute-done.20.near, ...), custom_call_target="tpu_custom_call" | custom-call | flops 905969664 | bytes 3145728 | tf_op jit(solution)/shard_map/window_stats/pallas_call | solution.py:110
  67.3 10.3 %collective-permute-done.31.far = bf16[2,384,512]{2,1,0:T(8,128)(2,1)} collective-permute-done((bf16[2,384,512]{2,1,0:T(8,128)(2,1)}, bf16[2,384,512]{2,1,0:T(8,128)(2,1)}, u32[]{:S(2)}, u32[]{:S(2)}) %collective-permute-start.31) | collective-permute-done | bytes 786464 | tf_op jit(solution)/shard_map/ppermute | solution.py:161
  77.6 4.9 %window_stats.9 = (f32[8,384]{1,0:T(8,128)S(1)}, f32[8,384]{1,0:T(8,128)S(1)}, f32[8,384]{1,0:T(8,128)S(1)}) custom-call(f32[9,384]{1,0:T(8,128)S(1)} %bitcast.24, bf16[1,384,3072]{2,1,0:T(8,128)(2,1)S(1)} %copy-done, bf16[1,384,3072]{2,1,0:T(8,128)(2,1)S(1)} %copy-done.1, bf16[2,384,512]{2,1,0:T(8,128)(2,1)} %collective-permute-done.30.near, ...), custom_call_target="tpu_custom_call" | custom-call | flops 905969664 | bytes 3145728 | tf_op jit(solution)/shard_map/window_stats/pallas_call | solution.py:110
  82.6 9.4 %collective-permute-done.41.far = bf16[2,384,512]{2,1,0:T(8,128)(2,1)} collective-permute-done((bf16[2,384,512]{2,1,0:T(8,128)(2,1)}, bf16[2,384,512]{2,1,0:T(8,128)(2,1)}, u32[]{:S(2)}, u32[]{:S(2)}) %collective-permute-start.41) | collective-permute-done | bytes 786464 | tf_op jit(solution)/shard_map/ppermute | solution.py:161
  92.0 4.9 %window_stats.10 = (f32[8,384]{1,0:T(8,128)S(1)}, f32[8,384]{1,0:T(8,128)S(1)}, f32[8,384]{1,0:T(8,128)S(1)}) custom-call(f32[9,384]{1,0:T(8,128)S(1)} %bitcast.25, bf16[1,384,3072]{2,1,0:T(8,128)(2,1)S(1)} %copy-done, bf16[1,384,3072]{2,1,0:T(8,128)(2,1)S(1)} %copy-done.1, bf16[2,384,512]{2,1,0:T(8,128)(2,1)} %collective-permute-done.40.near, ...), custom_call_target="tpu_custom_call" | custom-call | flops 905969664 | bytes 3145728 | tf_op jit(solution)/shard_map/window_stats/pallas_call | solution.py:110
  112.2 8.9 %window_grads.6 = (bf16[384,512]{1,0:T(8,128)(2,1)S(1)}, f32[384,512]{1,0:T(8,128)S(1)}, bf16[384,512]{1,0:T(8,128)(2,1)S(1)}, bf16[2,384,512]{2,1,0:T(8,128)(2,1)S(1)}) custom-call(f32[9,384]{1,0:T(8,128)S(1)} %bitcast.26, bf16[1,384,3072]{2,1,0:T(8,128)(2,1)S(1)} %copy-done, bf16[1,384,3072]{2,1,0:T(8,128)(2,1)S(1)} %copy-done.1, ...), custom_call_target="tpu_custom_call" | custom-call | flops 2264924160 | bytes 5505024 | tf_op jit(solution)/shard_map/window_grads/pallas_call | solution.py:132
  122.7 9.0 %window_grads.7 = (bf16[384,512]{1,0:T(8,128)(2,1)S(1)}, f32[384,512]{1,0:T(8,128)S(1)}, bf16[384,512]{1,0:T(8,128)(2,1)S(1)}, bf16[2,384,512]{2,1,0:T(8,128)(2,1)S(1)}) custom-call(f32[9,384]{1,0:T(8,128)S(1)} %bitcast.27, bf16[1,384,3072]{2,1,0:T(8,128)(2,1)S(1)} %copy-done, bf16[1,384,3072]{2,1,0:T(8,128)(2,1)S(1)} %copy-done.1, ...), custom_call_target="tpu_custom_call" | custom-call | flops 2264924160 | bytes 5505024 | tf_op jit(solution)/shard_map/window_grads/pallas_call | solution.py:132
  135.2 8.9 %window_grads.8 = (bf16[384,512]{1,0:T(8,128)(2,1)S(1)}, f32[384,512]{1,0:T(8,128)S(1)}, bf16[384,512]{1,0:T(8,128)(2,1)S(1)}, bf16[2,384,512]{2,1,0:T(8,128)(2,1)S(1)}) custom-call(f32[9,384]{1,0:T(8,128)S(1)} %bitcast.28, bf16[1,384,3072]{2,1,0:T(8,128)(2,1)S(1)} %copy-done, bf16[1,384,3072]{2,1,0:T(8,128)(2,1)S(1)} %copy-done.1, ...), custom_call_target="tpu_custom_call" | custom-call | flops 2264924160 | bytes 5505024 | tf_op jit(solution)/shard_map/window_grads/pallas_call | solution.py:132
  148.0 8.9 %window_grads.9 = (bf16[384,512]{1,0:T(8,128)(2,1)S(1)}, f32[384,512]{1,0:T(8,128)S(1)}, bf16[384,512]{1,0:T(8,128)(2,1)S(1)}, bf16[2,384,512]{2,1,0:T(8,128)(2,1)S(1)}) custom-call(f32[9,384]{1,0:T(8,128)S(1)} %bitcast.29, bf16[1,384,3072]{2,1,0:T(8,128)(2,1)S(1)} %copy-done, bf16[1,384,3072]{2,1,0:T(8,128)(2,1)S(1)} %copy-done.1, ...), custom_call_target="tpu_custom_call" | custom-call | flops 2264924160 | bytes 5505024 | tf_op jit(solution)/shard_map/window_grads/pallas_call | solution.py:132
  159.2 9.2 %window_grads.10 = (bf16[384,512]{1,0:T(8,128)(2,1)S(1)}, f32[384,512]{1,0:T(8,128)S(1)}, bf16[384,512]{1,0:T(8,128)(2,1)S(1)}, bf16[2,384,512]{2,1,0:T(8,128)(2,1)S(1)}) custom-call(f32[9,384]{1,0:T(8,128)S(1)} %bitcast.30, bf16[1,384,3072]{2,1,0:T(8,128)(2,1)S(1)} %copy-done, bf16[1,384,3072]{2,1,0:T(8,128)(2,1)S(1)} %copy-done.1, ...), custom_call_target="tpu_custom_call" | custom-call | flops 2264924160 | bytes 5505024 | tf_op jit(solution)/shard_map/window_grads/pallas_call | solution.py:132
  174.4 24.4 %collective-permute-done.37 = bf16[384,512]{1,0:T(8,128)(2,1)S(1)} collective-permute-done((bf16[384,512]{1,0:T(8,128)(2,1)S(1)}, bf16[384,512]{1,0:T(8,128)(2,1)S(1)}, u32[]{:S(2)}, u32[]{:S(2)}) %collective-permute-start.37) | collective-permute-done | bytes 393248 | tf_op jit(solution)/shard_map/ppermute | solution.py:161
  200.5 4.0 %window_stats.11 = (f32[8,384]{1,0:T(8,128)S(1)}, f32[8,384]{1,0:T(8,128)S(1)}, f32[8,384]{1,0:T(8,128)S(1)}) custom-call(f32[9,384]{1,0:T(8,128)S(1)} %bitcast.31, bf16[2,384,512]{2,1,0:T(8,128)(2,1)S(1)} %collective-permute-done.50.q_own.o_own, bf16[2,384,512]{2,1,0:T(8,128)(2,1)S(1)} %collective-permute-done.50.q_own.o_own, ...), custom_call_target="tpu_custom_call" | custom-call | flops 905969664 | bytes 3145728 | tf_op jit(solution)/shard_map/window_stats/pallas_call | solution.py:110
  208.8 2.9 collective-permute-done.55
  211.7 2.2 collective-permute-start.9
  215.4 2.9 collective-permute-done.18
  218.3 2.3 collective-permute-start.56
  220.7 6.1 %collective-permute-done.28 = bf16[1,384,512]{2,1,0:T(8,128)(2,1)S(1)} collective-permute-done((bf16[1,384,512]{2,1,0:T(8,128)(2,1)S(1)}, bf16[1,384,512]{2,1,0:T(8,128)(2,1)S(1)}, u32[]{:S(2)}, u32[]{:S(2)}) %collective-permute-start.28) | collective-permute-done | bytes 393248 | tf_op jit(solution)/shard_map/ppermute | solution.py:166
  226.8 3.2 collective-permute-start.57
  231.9 11.7 %collective-permute-done.9 = bf16[2,384,512]{2,1,0:T(8,128)(2,1)S(1)} collective-permute-done((bf16[2,384,512]{2,1,0:T(8,128)(2,1)S(1)}, bf16[2,384,512]{2,1,0:T(8,128)(2,1)S(1)}, u32[]{:S(2)}, u32[]{:S(2)}) %collective-permute-start.9) | collective-permute-done | bytes 786464 | tf_op jit(solution)/shard_map/ppermute | solution.py:166
  243.6 8.2 %window_grads.11 = (bf16[384,512]{1,0:T(8,128)(2,1)S(1)}, f32[384,512]{1,0:T(8,128)S(1)}, bf16[384,512]{1,0:T(8,128)(2,1)S(1)}, bf16[2,384,512]{2,1,0:T(8,128)(2,1)S(1)}) custom-call(f32[9,384]{1,0:T(8,128)S(1)} %bitcast.32, bf16[2,384,512]{2,1,0:T(8,128)(2,1)S(1)} %collective-permute-done.50.q_own.o_own, ...), custom_call_target="tpu_custom_call" | custom-call | flops 2264924160 | bytes 5505024 | tf_op jit(solution)/shard_map/window_grads/pallas_call | solution.py:132
  252.0 8.5 %collective-permute-done.19 = bf16[2,384,512]{2,1,0:T(8,128)(2,1)S(1)} collective-permute-done((bf16[2,384,512]{2,1,0:T(8,128)(2,1)S(1)}, bf16[2,384,512]{2,1,0:T(8,128)(2,1)S(1)}, u32[]{:S(2)}, u32[]{:S(2)}) %collective-permute-start.19) | collective-permute-done | bytes 786464 | tf_op jit(solution)/shard_map/ppermute | solution.py:166
  260.6 58.8 %collective-permute-done.38 = bf16[1,384,512]{2,1,0:T(8,128)(2,1)S(1)} collective-permute-done((bf16[1,384,512]{2,1,0:T(8,128)(2,1)S(1)}, bf16[1,384,512]{2,1,0:T(8,128)(2,1)S(1)}, u32[]{:S(2)}, u32[]{:S(2)}) %collective-permute-start.38) | collective-permute-done | bytes 393248 | tf_op jit(solution)/shard_map/ppermute | solution.py:166
  319.4 3.2 collective-permute-start.59
  322.9 5.0 %collective-permute-done.48 = bf16[1,384,512]{2,1,0:T(8,128)(2,1)S(1)} collective-permute-done((bf16[1,384,512]{2,1,0:T(8,128)(2,1)S(1)}, bf16[1,384,512]{2,1,0:T(8,128)(2,1)S(1)}, u32[]{:S(2)}, u32[]{:S(2)}) %collective-permute-start.48) | collective-permute-done | bytes 393248 | tf_op jit(solution)/shard_map/ppermute | solution.py:166
  328.0 3.0 collective-permute-done.59
  331.4 3.0 copy-done.6
  (162 shorter events, 59.3 us)
Async XLA Ops:
  5.0 22.0 %collective-permute-start.1 = (bf16[2,384,512]{2,1,0:T(8,128)(2,1)}, bf16[2,384,512]{2,1,0:T(8,128)(2,1)}, u32[]{:S(2)}, u32[]{:S(2)}) collective-permute-start(bf16[2,384,512]{2,1,0:T(8,128)(2,1)} %pad_maximum_fusion), channel_id=1, source_target_pairs={{0,28},{4,8},{8,4},{12,16},{16,12},{20,24},{24,20},{28,0},{1,29},{... | collective-permute-start | bytes 2359304 | tf_op jit(solution)/shard_map/ppermute | solution.py:161
  6.0 21.1 %collective-permute-start.10 = (bf16[2,384,512]{2,1,0:T(8,128)(2,1)}, bf16[2,384,512]{2,1,0:T(8,128)(2,1)}, u32[]{:S(2)}, u32[]{:S(2)}) collective-permute-start(bf16[2,384,512]{2,1,0:T(8,128)(2,1)} %pad_maximum_fusion.1), channel_id=1, source_target_pairs={{0,4},{4,0},{8,12},{12,8},{16,20},{20,16},{24,28},{28,24},{1,5},{5... | collective-permute-start | bytes 2359304 | tf_op jit(solution)/shard_map/ppermute | solution.py:156
  6.5 37.4 %collective-permute-start.11 = (bf16[2,384,512]{2,1,0:T(8,128)(2,1)}, bf16[2,384,512]{2,1,0:T(8,128)(2,1)}, u32[]{:S(2)}, u32[]{:S(2)}) collective-permute-start(bf16[2,384,512]{2,1,0:T(8,128)(2,1)} %pad_maximum_fusion.1), channel_id=1, source_target_pairs={{0,28},{4,8},{8,4},{12,16},{16,12},{20,24},{24,20},{28,0},{1,29},{... | collective-permute-start | bytes 2359304 | tf_op jit(solution)/shard_map/ppermute | solution.py:161
  10.5 33.4 %collective-permute-start.20 = (bf16[2,384,512]{2,1,0:T(8,128)(2,1)}, bf16[2,384,512]{2,1,0:T(8,128)(2,1)}, u32[]{:S(2)}, u32[]{:S(2)}) collective-permute-start(bf16[2,384,512]{2,1,0:T(8,128)(2,1)} %pad_maximum_fusion.2), channel_id=1, source_target_pairs={{0,4},{4,0},{8,12},{12,8},{16,20},{20,16},{24,28},{28,24},{1,5},{5... | collective-permute-start | bytes 2359304 | tf_op jit(solution)/shard_map/ppermute | solution.py:156
  12.4 48.4 %collective-permute-start.21 = (bf16[2,384,512]{2,1,0:T(8,128)(2,1)}, bf16[2,384,512]{2,1,0:T(8,128)(2,1)}, u32[]{:S(2)}, u32[]{:S(2)}) collective-permute-start(bf16[2,384,512]{2,1,0:T(8,128)(2,1)} %pad_maximum_fusion.2), channel_id=1, source_target_pairs={{0,28},{4,8},{8,4},{12,16},{16,12},{20,24},{24,20},{28,0},{1,29},{... | collective-permute-start | bytes 2359304 | tf_op jit(solution)/shard_map/ppermute | solution.py:161
  27.0 38.9 %collective-permute-start.30 = (bf16[2,384,512]{2,1,0:T(8,128)(2,1)}, bf16[2,384,512]{2,1,0:T(8,128)(2,1)}, u32[]{:S(2)}, u32[]{:S(2)}) collective-permute-start(bf16[2,384,512]{2,1,0:T(8,128)(2,1)} %pad_maximum_fusion.3), channel_id=1, source_target_pairs={{0,4},{4,0},{8,12},{12,8},{16,20},{20,16},{24,28},{28,24},{1,5},{5... | collective-permute-start | bytes 2359304 | tf_op jit(solution)/shard_map/ppermute | solution.py:156
  27.0 50.6 %collective-permute-start.31 = (bf16[2,384,512]{2,1,0:T(8,128)(2,1)}, bf16[2,384,512]{2,1,0:T(8,128)(2,1)}, u32[]{:S(2)}, u32[]{:S(2)}) collective-permute-start(bf16[2,384,512]{2,1,0:T(8,128)(2,1)} %pad_maximum_fusion.3), channel_id=1, source_target_pairs={{0,28},{4,8},{8,4},{12,16},{16,12},{20,24},{24,20},{28,0},{1,29},{... | collective-permute-start | bytes 2359304 | tf_op jit(solution)/shard_map/ppermute | solution.py:161
  43.9 38.6 %collective-permute-start.40 = (bf16[2,384,512]{2,1,0:T(8,128)(2,1)}, bf16[2,384,512]{2,1,0:T(8,128)(2,1)}, u32[]{:S(2)}, u32[]{:S(2)}) collective-permute-start(bf16[2,384,512]{2,1,0:T(8,128)(2,1)} %pad_maximum_fusion.4), channel_id=1, source_target_pairs={{0,4},{4,0},{8,12},{12,8},{16,20},{20,16},{24,28},{28,24},{1,5},{5... | collective-permute-start | bytes 2359304 | tf_op jit(solution)/shard_map/ppermute | solution.py:156
  43.9 48.1 %collective-permute-start.41 = (bf16[2,384,512]{2,1,0:T(8,128)(2,1)}, bf16[2,384,512]{2,1,0:T(8,128)(2,1)}, u32[]{:S(2)}, u32[]{:S(2)}) collective-permute-start(bf16[2,384,512]{2,1,0:T(8,128)(2,1)} %pad_maximum_fusion.4), channel_id=1, source_target_pairs={{0,28},{4,8},{8,4},{12,16},{16,12},{20,24},{24,20},{28,0},{1,29},{... | collective-permute-start | bytes 2359304 | tf_op jit(solution)/shard_map/ppermute | solution.py:161
  60.7 83.4 %collective-permute-start.50 = (bf16[2,384,512]{2,1,0:T(8,128)(2,1)S(1)}, bf16[2,384,512]{2,1,0:T(8,128)(2,1)S(1)}, u32[]{:S(2)}, u32[]{:S(2)}) collective-permute-start(bf16[2,384,512]{2,1,0:T(8,128)(2,1)S(1)} %pad_maximum_fusion.5), channel_id=1, source_target_pairs={{1,0},{2,1},{3,2},{0,3},{5,4},{6,5},{7,6},{4,7},{9,8},{10,9},{11,1... | collective-permute-start | bytes 2359304 | tf_op jit(solution)/shard_map/ppermute | solution.py:166
  65.9 78.3 %collective-permute-start.53 = (bf16[2,384,512]{2,1,0:T(8,128)(2,1)S(1)}, bf16[2,384,512]{2,1,0:T(8,128)(2,1)S(1)}, u32[]{:S(2)}, u32[]{:S(2)}) collective-permute-start(bf16[2,384,512]{2,1,0:T(8,128)(2,1)S(1)} %pad_maximum_fusion.6), channel_id=1, source_target_pairs={{1,0},{2,1},{3,2},{0,3},{5,4},{6,5},{7,6},{4,7},{9,8},{10,9},{11,1... | collective-permute-start | bytes 2359304 | tf_op jit(solution)/shard_map/ppermute | solution.py:166
  77.6 19.3 %collective-permute-start.2 = (f32[8,384]{1,0:T(8,128)S(1)}, f32[8,384]{1,0:T(8,128)S(1)}, u32[]{:S(2)}, u32[]{:S(2)}) collective-permute-start(f32[8,384]{1,0:T(8,128)S(1)} %get-tuple-element.48), channel_id=1, source_target_pairs={{0,4},{4,0},{8,12},{12,8},{16,20},{20,16},{24,28},{28,24},{1,5},{5... | collective-permute-start | bytes 36872 | tf_op jit(solution)/shard_map/ppermute | solution.py:156
  82.5 16.1 %collective-permute-start.3 = (f32[8,384]{1,0:T(8,128)S(1)}, f32[8,384]{1,0:T(8,128)S(1)}, u32[]{:S(2)}, u32[]{:S(2)}) collective-permute-start(f32[8,384]{1,0:T(8,128)S(1)} %get-tuple-element.49), channel_id=1, source_target_pairs={{0,28},{4,8},{8,4},{12,16},{16,12},{20,24},{24,20},{28,0},{1,29},{... | collective-permute-start | bytes 36872 | tf_op jit(solution)/shard_map/ppermute | solution.py:161
  112.2 19.4 %collective-permute-start.24 = (f32[8,384]{1,0:T(8,128)S(1)}, f32[8,384]{1,0:T(8,128)S(1)}, u32[]{:S(2)}, u32[]{:S(2)}) collective-permute-start(f32[8,384]{1,0:T(8,128)S(1)} %pad_maximum_fusion.9.st_own), channel_id=1, source_target_pairs={{0,4},{4,0},{8,12},{12,8},{16,20},{20,16},{24,28},{28,24},{1,5},{5... | collective-permute-start | bytes 36872 | tf_op jit(solution)/shard_map/ppermute | solution.py:156
  122.7 23.8 %collective-permute-start.34 = (f32[8,384]{1,0:T(8,128)S(1)}, f32[8,384]{1,0:T(8,128)S(1)}, u32[]{:S(2)}, u32[]{:S(2)}) collective-permute-start(f32[8,384]{1,0:T(8,128)S(1)} %pad_maximum_fusion.10.st_own), channel_id=1, source_target_pairs={{0,4},{4,0},{8,12},{12,8},{16,20},{20,16},{24,28},{28,24},{1,5},{5... | collective-permute-start | bytes 36872 | tf_op jit(solution)/shard_map/ppermute | solution.py:156
  133.8 25.4 %collective-permute-start.7 = (bf16[384,512]{1,0:T(8,128)(2,1)S(1)}, bf16[384,512]{1,0:T(8,128)(2,1)S(1)}, u32[]{:S(2)}, u32[]{:S(2)}) collective-permute-start(bf16[384,512]{1,0:T(8,128)(2,1)S(1)} %get-tuple-element.52), channel_id=1, source_target_pairs={{0,28},{4,8},{8,4},{12,16},{16,12},{20,24},{24,20},{28,0},{1,29},{... | collective-permute-start | bytes 1179656 | tf_op jit(solution)/shard_map/ppermute | solution.py:161
  146.4 21.9 %collective-permute-start.6 = (bf16[384,512]{1,0:T(8,128)(2,1)S(1)}, bf16[384,512]{1,0:T(8,128)(2,1)S(1)}, u32[]{:S(2)}, u32[]{:S(2)}) collective-permute-start(bf16[384,512]{1,0:T(8,128)(2,1)S(1)} %get-tuple-element.51), channel_id=1, source_target_pairs={{0,4},{4,0},{8,12},{12,8},{16,20},{20,16},{24,28},{28,24},{1,5},{5... | collective-permute-start | bytes 1179656 | tf_op jit(solution)/shard_map/ppermute | solution.py:156
  146.4 22.3 %collective-permute-start.17 = (bf16[384,512]{1,0:T(8,128)(2,1)S(1)}, bf16[384,512]{1,0:T(8,128)(2,1)S(1)}, u32[]{:S(2)}, u32[]{:S(2)}) collective-permute-start(bf16[384,512]{1,0:T(8,128)(2,1)S(1)} %get-tuple-element.59), channel_id=1, source_target_pairs={{0,28},{4,8},{8,4},{12,16},{16,12},{20,24},{24,20},{28,0},{1,29},{... | collective-permute-start | bytes 1179656 | tf_op jit(solution)/shard_map/ppermute | solution.py:161
  168.3 30.7 %collective-permute-start.51 = (bf16[2,384,512]{2,1,0:T(8,128)(2,1)S(1)}, bf16[2,384,512]{2,1,0:T(8,128)(2,1)S(1)}, u32[]{:S(2)}, u32[]{:S(2)}) collective-permute-start(bf16[2,384,512]{2,1,0:T(8,128)(2,1)S(1)} %collective-permute-done.50.q_own.o_own), channel_id=1, source_target_pairs={{0,4},{4,0},{8,12},{12,8},{16,20},{20,16},{24,28},{28,24},{1,5},{5... | collective-permute-start | bytes 2359304 | tf_op jit(solution)/shard_map/ppermute | solution.py:156
  168.7 31.6 %collective-permute-start.52 = (bf16[2,384,512]{2,1,0:T(8,128)(2,1)S(1)}, bf16[2,384,512]{2,1,0:T(8,128)(2,1)S(1)}, u32[]{:S(2)}, u32[]{:S(2)}) collective-permute-start(bf16[2,384,512]{2,1,0:T(8,128)(2,1)S(1)} %collective-permute-done.50.q_own.o_own), channel_id=1, source_target_pairs={{0,28},{4,8},{8,4},{12,16},{16,12},{20,24},{24,20},{28,0},{1,29},{... | collective-permute-start | bytes 2359304 | tf_op jit(solution)/shard_map/ppermute | solution.py:161
  170.3 28.5 %collective-permute-start.37 = (bf16[384,512]{1,0:T(8,128)(2,1)S(1)}, bf16[384,512]{1,0:T(8,128)(2,1)S(1)}, u32[]{:S(2)}, u32[]{:S(2)}) collective-permute-start(bf16[384,512]{1,0:T(8,128)(2,1)S(1)} %get-tuple-element.73), channel_id=1, source_target_pairs={{0,28},{4,8},{8,4},{12,16},{16,12},{20,24},{24,20},{28,0},{1,29},{... | collective-permute-start | bytes 1179656 | tf_op jit(solution)/shard_map/ppermute | solution.py:161
  172.5 26.4 %collective-permute-start.36 = (bf16[384,512]{1,0:T(8,128)(2,1)S(1)}, bf16[384,512]{1,0:T(8,128)(2,1)S(1)}, u32[]{:S(2)}, u32[]{:S(2)}) collective-permute-start(bf16[384,512]{1,0:T(8,128)(2,1)S(1)} %get-tuple-element.72), channel_id=1, source_target_pairs={{0,4},{4,0},{8,12},{12,8},{16,20},{20,16},{24,28},{28,24},{1,5},{5... | collective-permute-start | bytes 1179656 | tf_op jit(solution)/shard_map/ppermute | solution.py:156
  172.5 32.6 %collective-permute-start.47 = (bf16[384,512]{1,0:T(8,128)(2,1)S(1)}, bf16[384,512]{1,0:T(8,128)(2,1)S(1)}, u32[]{:S(2)}, u32[]{:S(2)}) collective-permute-start(bf16[384,512]{1,0:T(8,128)(2,1)S(1)} %get-tuple-element.80), channel_id=1, source_target_pairs={{0,28},{4,8},{8,4},{12,16},{16,12},{20,24},{24,20},{28,0},{1,29},{... | collective-permute-start | bytes 1179656 | tf_op jit(solution)/shard_map/ppermute | solution.py:161
  199.1 19.2 %collective-permute-start.18 = (bf16[1,384,512]{2,1,0:T(8,128)(2,1)S(1)}, bf16[1,384,512]{2,1,0:T(8,128)(2,1)S(1)}, u32[]{:S(2)}, u32[]{:S(2)}) collective-permute-start(bf16[1,384,512]{2,1,0:T(8,128)(2,1)S(1)} %fusion.1), channel_id=1, source_target_pairs={{1,0},{2,1},{3,2},{0,3},{5,4},{6,5},{7,6},{4,7},{9,8},{10,9},{11,1... | collective-permute-start | bytes 1179656 | tf_op jit(solution)/shard_map/ppermute | solution.py:166
  200.3 26.5 %collective-permute-start.28 = (bf16[1,384,512]{2,1,0:T(8,128)(2,1)S(1)}, bf16[1,384,512]{2,1,0:T(8,128)(2,1)S(1)}, u32[]{:S(2)}, u32[]{:S(2)}) collective-permute-start(bf16[1,384,512]{2,1,0:T(8,128)(2,1)S(1)} %fusion.2), channel_id=1, source_target_pairs={{1,0},{2,1},{3,2},{0,3},{5,4},{6,5},{7,6},{4,7},{9,8},{10,9},{11,1... | collective-permute-start | bytes 1179656 | tf_op jit(solution)/shard_map/ppermute | solution.py:166
  211.7 31.9 %collective-permute-start.9 = (bf16[2,384,512]{2,1,0:T(8,128)(2,1)S(1)}, bf16[2,384,512]{2,1,0:T(8,128)(2,1)S(1)}, u32[]{:S(2)}, u32[]{:S(2)}) collective-permute-start(bf16[2,384,512]{2,1,0:T(8,128)(2,1)S(1)} %get-tuple-element.53), channel_id=1, source_target_pairs={{1,0},{2,1},{3,2},{0,3},{5,4},{6,5},{7,6},{4,7},{9,8},{10,9},{11,1... | collective-permute-start | bytes 2359304 | tf_op jit(solution)/shard_map/ppermute | solution.py:166
  213.9 46.5 %collective-permute-start.19 = (bf16[2,384,512]{2,1,0:T(8,128)(2,1)S(1)}, bf16[2,384,512]{2,1,0:T(8,128)(2,1)S(1)}, u32[]{:S(2)}, u32[]{:S(2)}) collective-permute-start(bf16[2,384,512]{2,1,0:T(8,128)(2,1)S(1)} %get-tuple-element.60), channel_id=1, source_target_pairs={{1,0},{2,1},{3,2},{0,3},{5,4},{6,5},{7,6},{4,7},{9,8},{10,9},{11,1... | collective-permute-start | bytes 2359304 | tf_op jit(solution)/shard_map/ppermute | solution.py:166
  214.3 108.3 %collective-permute-start.29 = (bf16[2,384,512]{2,1,0:T(8,128)(2,1)S(1)}, bf16[2,384,512]{2,1,0:T(8,128)(2,1)S(1)}, u32[]{:S(2)}, u32[]{:S(2)}) collective-permute-start(bf16[2,384,512]{2,1,0:T(8,128)(2,1)S(1)} %get-tuple-element.67), channel_id=1, source_target_pairs={{1,0},{2,1},{3,2},{0,3},{5,4},{6,5},{7,6},{4,7},{9,8},{10,9},{11,1... | collective-permute-start | bytes 2359304 | tf_op jit(solution)/shard_map/ppermute | solution.py:166
  230.1 92.7 %collective-permute-start.39 = (bf16[2,384,512]{2,1,0:T(8,128)(2,1)S(1)}, bf16[2,384,512]{2,1,0:T(8,128)(2,1)S(1)}, u32[]{:S(2)}, u32[]{:S(2)}) collective-permute-start(bf16[2,384,512]{2,1,0:T(8,128)(2,1)S(1)} %get-tuple-element.74), channel_id=1, source_target_pairs={{1,0},{2,1},{3,2},{0,3},{5,4},{6,5},{7,6},{4,7},{9,8},{10,9},{11,1... | collective-permute-start | bytes 2359304 | tf_op jit(solution)/shard_map/ppermute | solution.py:166
  231.7 96.2 %collective-permute-start.49 = (bf16[2,384,512]{2,1,0:T(8,128)(2,1)S(1)}, bf16[2,384,512]{2,1,0:T(8,128)(2,1)S(1)}, u32[]{:S(2)}, u32[]{:S(2)}) collective-permute-start(bf16[2,384,512]{2,1,0:T(8,128)(2,1)S(1)} %get-tuple-element.81), channel_id=1, source_target_pairs={{1,0},{2,1},{3,2},{0,3},{5,4},{6,5},{7,6},{4,7},{9,8},{10,9},{11,1... | collective-permute-start | bytes 2359304 | tf_op jit(solution)/shard_map/ppermute | solution.py:166
  243.6 75.8 %collective-permute-start.38 = (bf16[1,384,512]{2,1,0:T(8,128)(2,1)S(1)}, bf16[1,384,512]{2,1,0:T(8,128)(2,1)S(1)}, u32[]{:S(2)}, u32[]{:S(2)}) collective-permute-start(bf16[1,384,512]{2,1,0:T(8,128)(2,1)S(1)} %fusion.3), channel_id=1, source_target_pairs={{1,0},{2,1},{3,2},{0,3},{5,4},{6,5},{7,6},{4,7},{9,8},{10,9},{11,1... | collective-permute-start | bytes 1179656 | tf_op jit(solution)/shard_map/ppermute | solution.py:166
  260.5 67.4 %collective-permute-start.48 = (bf16[1,384,512]{2,1,0:T(8,128)(2,1)S(1)}, bf16[1,384,512]{2,1,0:T(8,128)(2,1)S(1)}, u32[]{:S(2)}, u32[]{:S(2)}) collective-permute-start(bf16[1,384,512]{2,1,0:T(8,128)(2,1)S(1)} %fusion.4), channel_id=1, source_target_pairs={{1,0},{2,1},{3,2},{0,3},{5,4},{6,5},{7,6},{4,7},{9,8},{10,9},{11,1... | collective-permute-start | bytes 1179656 | tf_op jit(solution)/shard_map/ppermute | solution.py:166
  (38 other events, 364.3 us)
